TPU v7x, 32 devices: a whole 2x2x4 slice. The times are simulated.
32 devices in a mesh: energy: 8 (over z, x), section: 4 (over y, core).
Axes of the slice: x: 2, y: 2, z: 4, core: 2. Of those that a mesh axis runs over, the one named last changes fastest.
Arguments:
- propagator: bfloat16 [8, 4, 2, 384, 384], P('energy', 'section')
- forward_source: bfloat16 [8, 4, 384, 128], P('energy', 'section'), may hold values from -6 to 6
- backward_source: bfloat16 [8, 4, 384, 128], P('energy', 'section'), may hold values from -6 to 6
- left_orbital: int32 [32768], P('section'), may hold values from 0 to 1535, as said below
- right_orbital: int32 [32768], P('section'), may hold values from 0 to 1535
- phonon_shift: int32 [8], replicated, may hold values from -6 to 6
- coupling: float32 [8, 32768], P(None, 'section'), may hold values from 0.1 to 1
Outputs:
- self_energy: float32 [2, 8, 32768], P(None, 'energy', 'section')
Inputs may be any that keep to these rules, and one draw needn't show every extreme that they name: left_orbital[p] and right_orbital[p] are orbitals of section p // 8192: both lie from (p // 8192) * 384 to that plus 1 * 384 - 1, and they differ by at most 24.
All inputs are finite; a program needn't handle non-finite values.
Results may differ from a plain program's by a relative error of at most 0.022.
Values may be sent and summed in bfloat16 or wider, within the bound.
A program may use at most 64 MiB of HBM per device.

v0:
```python
import jax
import jax.numpy as jnp
from jax import lax
from jax.sharding import PartitionSpec as P


def passed_along(value, axis, steps):
    count = lax.axis_size(axis)
    leading, last = (max(0, -steps), min(count, count - steps))
    return lax.ppermute(value, axis, [(source, source + steps) for source in range(leading, last)])


def as_sent(shard):

    def short(part):
        return part.astype(jnp.bfloat16) if part.dtype == jnp.float32 else part

    return jax.tree.map(short, shard)


def complex_product(matrix, columns, adjoint):
    half = columns.shape[1] // 2
    if adjoint:
        product = jnp.einsum("cji,jn->cin", matrix, columns, preferred_element_type=jnp.float32)
        real_part = product[0, :, :half] + product[1, :, half:]
        imag_part = product[0, :, half:] - product[1, :, :half]
    else:
        product = jnp.einsum("cij,jn->cin", matrix, columns, preferred_element_type=jnp.float32)
        real_part = product[0, :, :half] - product[1, :, half:]
        imag_part = product[0, :, half:] + product[1, :, :half]
    return jnp.concatenate([real_part, imag_part], axis=1)


def as_pair(joined):
    width = joined.shape[0]
    return jnp.stack([joined[:, :width], joined[:, width:]])


def section_maps(blocks, forward_src, backward_src):
    count = blocks.shape[0]
    composite = jnp.concatenate([blocks[0, 0], blocks[0, 1]], axis=1)
    forward_part = forward_src[0]
    backward_part = backward_src[count - 1]
    return (composite, forward_part, backward_part)


def forward_pass(blocks, sources, start_state):
    current = start_state
    current = (complex_product(blocks[0], current, False) + sources[0]).astype(jnp.bfloat16)
    results = [current]
    return jnp.stack(results)


def backward_pass(blocks, sources, start_state):
    current = start_state
    results = [None] * blocks.shape[0]
    current = (complex_product(blocks[0], current, True) + sources[0]).astype(jnp.bfloat16)
    results[0] = current
    return jnp.stack(results)


def apply_forward(matrix, current, vector):
    return (complex_product(as_pair(matrix), current, False) + vector).astype(jnp.bfloat16)


def apply_backward(matrix, current, vector):
    return (complex_product(as_pair(matrix), current, True) + vector).astype(jnp.bfloat16)


def lesser(field_rows, adjoint_rows, left_index, right_index, modes):
    left_rows = jnp.take(field_rows, left_index, axis=0)
    right_rows = jnp.take(adjoint_rows, right_index, axis=0)
    first_real = jnp.einsum(
        "pr,pr->p", left_rows[:, :modes], right_rows[:, :modes], preferred_element_type=jnp.float32
    )
    first_imag = jnp.einsum(
        "pr,pr->p", left_rows[:, modes:], right_rows[:, modes:], preferred_element_type=jnp.float32
    )
    cross_one = jnp.einsum(
        "pr,pr->p", left_rows[:, modes:], right_rows[:, :modes], preferred_element_type=jnp.float32
    )
    cross_two = jnp.einsum(
        "pr,pr->p", left_rows[:, :modes], right_rows[:, modes:], preferred_element_type=jnp.float32
    )
    return jnp.stack([first_real + first_imag, cross_one - cross_two]) * modes ** (-0.5)


def shifted_sum(portion, own_energy, phonon_shift, coupling):
    count = portion.shape[1]
    positions = jnp.arange(count, dtype=jnp.int32)
    summed = jnp.zeros((portion.shape[0], own_energy.shape[0], portion.shape[2]), jnp.float32)
    for k in range(phonon_shift.shape[0]):
        selector = (positions[None, :] == (own_energy - phonon_shift[k])[:, None]).astype(
            jnp.float32
        )
        moved = jnp.einsum("ef,cfp->cep", selector, portion, precision=lax.Precision.HIGHEST)
        summed = summed + coupling[k][None, None, :] * moved
    return summed


def on_device(
    propagator, forward_source, backward_source, left_orbital, right_orbital, phonon_shift, coupling
):
    slab_count = propagator.shape[1]
    orbitals = propagator.shape[3]
    modes = forward_source.shape[3] // 2
    composite, forward_part, backward_part = jax.vmap(section_maps)(
        propagator, forward_source, backward_source
    )
    relay_turns = lax.axis_size("section") - 1

    def forward_turn(turn_index, current):
        outgoing = jax.vmap(apply_forward)(composite, current, forward_part)
        return passed_along(outgoing, "section", 1)

    def backward_turn(turn_index, current):
        outgoing = jax.vmap(apply_backward)(composite, current, backward_part)
        return passed_along(outgoing, "section", -1)

    incoming = lax.fori_loop(0, relay_turns, forward_turn, jnp.zeros_like(forward_part))
    returning = lax.fori_loop(0, relay_turns, backward_turn, jnp.zeros_like(backward_part))
    fields = jax.vmap(forward_pass)(propagator, forward_source, incoming)
    adjoints = jax.vmap(backward_pass)(propagator, backward_source, returning)
    section_base = lax.axis_index("section") * (slab_count * orbitals)
    left_local = left_orbital - section_base
    right_local = right_orbital - section_base

    def pair_values(field, adjoint_field):
        return lesser(
            field.reshape(-1, 2 * modes),
            adjoint_field.reshape(-1, 2 * modes),
            left_local,
            right_local,
            modes,
        )

    lesser_part = jnp.transpose(jax.vmap(pair_values)(fields, adjoints), (1, 0, 2))
    regrouped = lax.all_to_all(
        as_sent(lesser_part), "energy", split_axis=2, concat_axis=1, tiled=True
    ).astype(lesser_part.dtype)
    block_pairs = regrouped.shape[2]
    all_count = regrouped.shape[1]
    block_start = lax.axis_index("energy") * block_pairs
    coupling_block = lax.dynamic_slice_in_dim(coupling, block_start, block_pairs, 1)
    block_result = shifted_sum(
        regrouped, jnp.arange(all_count, dtype=jnp.int32), phonon_shift, coupling_block
    )
    self_energy = lax.all_to_all(
        as_sent(block_result), "energy", split_axis=1, concat_axis=2, tiled=True
    ).astype(block_result.dtype)
    return self_energy


def solution(mesh):
    placed = (
        P("energy", "section", None, None, None),
        P("energy", "section", None, None),
        P("energy", "section", None, None),
        P("section"),
        P("section"),
        P(),
        P(None, "section"),
    )
    return jax.shard_map(
        on_device,
        mesh=mesh,
        in_specs=placed,
        out_specs=P(None, "energy", "section"),
        check_vma=False,
    )
```

profile of v0, /device:TPU:0, one launch (start us, length us, event | category | flops | bytes accessed | tf_op | source)
XLA Modules:
  0.0 214.2 jit_solution(8793218675030848775)
XLA Ops:
  0.0 0.8 fusion.44
  0.8 0.8 compare_and_fusion
  1.6 1.1 slice_bitcast_fusion.5
  2.7 1.0 copy.29
  3.7 0.1 pad_maximum_fusion
  3.8 16.9 %while.25 = (s32[]{:T(128)}, bf16[1,384,128]{1,2,0:T(8,128)(2,1)S(1)}, bf16[2,1,384,384]{3,2,0,1:T(8,128)(2,1)S(1)}, bf16[1,384,128]{1,2,0:T(8,128)(2,1)S(1)}, s32[]{:T(128)}) while((s32[]{:T(128)}, bf16[1,384,128]{1,2,0:T(8,128)(2,1)S(1)}, bf16[2,1,384,384]{3,2,0,1:T(8,128)(2,1)S(1)}, bf16[1,384,128]{1,2,0:T(8,128)(2,1)S(1)}, s32[]{:T(128)}) %tuple.81), condition=%wide.region_3.5_spmd, body=%wide.region_2.4_spmd.sunk | while | flops 75743232 | bytes 2457701 | solution.py:121
  3.9 0.3 convolution_bitcast_fusion.7
  4.2 1.3 collective-permute-start.1
  5.5 1.9 collective-permute-done.1
  7.4 0.3 convolution_bitcast_fusion.7
  7.7 1.3 collective-permute-start.1
  9.0 5.5 %collective-permute-done.1 = bf16[1,384,128]{1,2,0:T(8,128)(2,1)S(1)} collective-permute-done((bf16[1,384,128]{1,2,0:T(8,128)(2,1)S(1)}, bf16[1,384,128]{1,2,0:T(8,128)(2,1)S(1)}, u32[]{:S(2)}, u32[]{:S(2)}) %collective-permute-start.1) | collective-permute-done | bytes 98336 | tf_op jit(solution)/shard_map/while/body/eval_jaxpr/ppermute | solution.py:10
  14.5 0.3 convolution_bitcast_fusion.7
  14.8 1.3 collective-permute-start.1
  16.1 4.6 %collective-permute-done.1 = bf16[1,384,128]{1,2,0:T(8,128)(2,1)S(1)} collective-permute-done((bf16[1,384,128]{1,2,0:T(8,128)(2,1)S(1)}, bf16[1,384,128]{1,2,0:T(8,128)(2,1)S(1)}, u32[]{:S(2)}, u32[]{:S(2)}) %collective-permute-start.1) | collective-permute-done | bytes 98336 | tf_op jit(solution)/shard_map/while/body/eval_jaxpr/ppermute | solution.py:10
  20.7 0.3 convolution_bitcast_fusion.2
  21.1 0.1 copy.30
  21.2 0.4 copy-done.1
  21.6 0.1 copy.27
  21.8 16.7 %while.24 = (s32[]{:T(128)}, bf16[1,384,128]{1,2,0:T(8,128)(2,1)S(1)}, bf16[2,1,384,384]{3,2,0,1:T(8,128)(2,1)S(1)}, bf16[1,384,128]{1,2,0:T(8,128)(2,1)S(1)}, s32[]{:T(128)}) while((s32[]{:T(128)}, bf16[1,384,128]{1,2,0:T(8,128)(2,1)S(1)}, bf16[2,1,384,384]{3,2,0,1:T(8,128)(2,1)S(1)}, bf16[1,384,128]{1,2,0:T(8,128)(2,1)S(1)}, s32[]{:T(128)}) %tuple.82), condition=%wide.region_1.0_spmd, body=%wide.region_0.0_spmd.sunk | while | flops 75743232 | bytes 2457701 | solution.py:120
  21.8 0.3 convolution_bitcast_fusion.6
  22.2 5.1 %collective-permute-start = (bf16[1,384,128]{1,2,0:T(8,128)(2,1)S(1)}, bf16[1,384,128]{1,2,0:T(8,128)(2,1)S(1)}, u32[]{:S(2)}, u32[]{:S(2)}) collective-permute-start(bf16[1,384,128]{1,2,0:T(8,128)(2,1)S(1)} %fusion.90), channel_id=1, source_target_pairs={{0,1},{1,2},{2,3},{4,5},{5,6},{6,7},{8,9},{9,10},{10,11},{12,13},{... | collective-permute-start | bytes 294920 | tf_op jit(solution)/shard_map/while/body/eval_jaxpr/ppermute | solution.py:10
  27.3 0.9 collective-permute-done
  28.2 0.3 convolution_bitcast_fusion.6
  28.6 2.6 %collective-permute-start = (bf16[1,384,128]{1,2,0:T(8,128)(2,1)S(1)}, bf16[1,384,128]{1,2,0:T(8,128)(2,1)S(1)}, u32[]{:S(2)}, u32[]{:S(2)}) collective-permute-start(bf16[1,384,128]{1,2,0:T(8,128)(2,1)S(1)} %fusion.90), channel_id=1, source_target_pairs={{0,1},{1,2},{2,3},{4,5},{5,6},{6,7},{8,9},{9,10},{10,11},{12,13},{... | collective-permute-start | bytes 294920 | tf_op jit(solution)/shard_map/while/body/eval_jaxpr/ppermute | solution.py:10
  31.3 0.9 collective-permute-done
  32.2 0.3 convolution_bitcast_fusion.6
  32.6 5.0 %collective-permute-start = (bf16[1,384,128]{1,2,0:T(8,128)(2,1)S(1)}, bf16[1,384,128]{1,2,0:T(8,128)(2,1)S(1)}, u32[]{:S(2)}, u32[]{:S(2)}) collective-permute-start(bf16[1,384,128]{1,2,0:T(8,128)(2,1)S(1)} %fusion.90), channel_id=1, source_target_pairs={{0,1},{1,2},{2,3},{4,5},{5,6},{6,7},{8,9},{9,10},{10,11},{12,13},{... | collective-permute-start | bytes 294920 | tf_op jit(solution)/shard_map/while/body/eval_jaxpr/ppermute | solution.py:10
  37.6 0.9 collective-permute-done
  38.5 0.3 convolution_bitcast_fusion.3
  38.9 0.1 copy.28
  39.0 29.4 %gather_fusion.1 = bf16[8192,128]{1,0:T(8,128)(2,1)} fusion(bf16[384,128]{1,0:T(8,128)(2,1)S(1)} %copy.30, s32[8192]{0:T(1024)S(1)} %get-tuple-element.173), kind=kCustom, calls=%fused_computation.1.clone | custom fusion | bytes 4227072 | tf_op jit(solution)/shard_map/vmap(jit(_take))/gather | solution.py:72
  68.4 5.8 %bitcast_select_fusion = bf16[1,8192,128]{2,1,0:T(8,128)(2,1)S(1)} fusion(bf16[8192,128]{1,0:T(8,128)(2,1)} %gather_fusion.1, pred[8192]{0:T(1024)(128)(4,1)S(1)} %get-tuple-element.170), kind=kLoop, calls=%fused_computation.32 | loop fusion | flops 1048576 | bytes 4202496 | tf_op jit(solution)/shard_map/vmap(jit(_take))/select_n | solution.py:72
  74.2 29.4 %gather_fusion = bf16[8192,128]{1,0:T(8,128)(2,1)} fusion(bf16[384,128]{1,0:T(8,128)(2,1)S(1)} %copy.28, s32[8192]{0:T(1024)S(1)} %get-tuple-element.172), kind=kCustom, calls=%fused_computation.clone | custom fusion | bytes 4227072 | tf_op jit(solution)/shard_map/vmap(jit(_take))/gather | solution.py:71
  103.6 5.8 %bitcast_select_fusion.1 = bf16[1,8192,128]{2,1,0:T(8,128)(2,1)S(1)} fusion(bf16[8192,128]{1,0:T(8,128)(2,1)} %gather_fusion, pred[8192]{0:T(1024)(128)(4,1)S(1)} %get-tuple-element.171), kind=kLoop, calls=%fused_computation.33 | loop fusion | flops 1048576 | bytes 4202496 | tf_op jit(solution)/shard_map/vmap(jit(_take))/select_n | solution.py:71
  109.5 6.1 %fusion.12 = (f32[8192]{0:T(1024)S(1)}, f32[8192]{0:T(1024)S(1)}, f32[8192]{0:T(1024)S(1)}, f32[8192]{0:T(1024)S(1)}) fusion(bf16[1,8192,128]{2,1,0:T(8,128)(2,1)S(1)} %bitcast_select_fusion.1, bf16[1,8192,128]{2,1,0:T(8,128)(2,1)S(1)} %bitcast_select_fusion), kind=kLoop, calls=%fused_computation.26 | loop fusion | flops 6258688 | bytes 4325376 | tf_op jit(solution)/shard_map/vmap(pr,pr->p)/dot_general | solution.py:76
  115.6 0.1 fusion.35
  115.7 6.8 %copy.33 = bf16[2,1,8192]{0,1,2:T(2,128)(2,1)} copy(bf16[2,1,8192]{2,0,1:T(2,128)(2,1)S(1)} %fusion.35) | data formatting | bytes 65536 | tf_op jit(solution)/shard_map/convert_element_type | solution.py:16
  122.5 0.5 broadcast.86
  123.0 45.4 %reduce.8 = bf16[8192,2]{1,0:T(8,128)(2,1)S(1)} reduce(bf16[8192,1,2]{2,1,0:T(2,128)(2,1)} %bitcast.183, bf16[]{:T(256)} %broadcast.86), dimensions={1}, to_apply=%bitcast.165.reduce_sub_computation | reduce | bytes 65538
  168.5 3.8 %reshape.584 = bf16[8,2,1024]{2,1,0:T(2,128)(2,1)} reshape(bf16[8192,2]{1,0:T(8,128)(2,1)S(1)} %reduce.8) | data formatting | bytes 65536
  172.3 5.8 %all-to-all-start = ((bf16[8,2,1024]{2,1,0:T(2,128)(2,1)}), bf16[8,2,1024]{2,1,0:T(2,128)(2,1)S(1)}, u32[]{:S(2)}, u32[]{:S(2)}) async-start(bf16[8,2,1024]{2,1,0:T(2,128)(2,1)} %reshape.584), calls=%async_computation | async-start | bytes 65536 | tf_op jit(solution)/shard_map/all_to_all | solution.py:138
  178.1 0.7 fusion.78
  178.8 0.6 iota_subtract_fusion.1
  179.4 0.6 iota_subtract_fusion.2
  180.0 0.7 iota_subtract_fusion.3
  180.7 0.6 iota_subtract_fusion.4
  181.3 0.7 iota_subtract_fusion.5
  181.9 0.6 iota_subtract_fusion.6
  182.6 0.6 iota_subtract_fusion
  183.2 1.2 constant_dynamic-slice_fusion
  184.4 0.6 iota_subtract_fusion.7
  185.1 6.2 %reshape.585 = bf16[8192,1,2]{2,1,0:T(2,128)(2,1)} reshape(bf16[8,2,1024]{2,1,0:T(2,128)(2,1)S(1)} %all-to-all-done) | data formatting | bytes 65536
  191.3 8.1 %copy.34 = bf16[2,1,8192]{2,0,1:T(2,128)(2,1)S(1)} copy(bf16[2,1,8192]{0,1,2:T(2,128)(2,1)} %bitcast.184) | data formatting | bytes 65536 | tf_op jit(solution)/shard_map/all_to_all | solution.py:138
  199.4 0.2 convolution_multiply_fusion.1
  199.6 0.2 convolution_multiply_fusion.2
  199.8 0.2 convolution_multiply_fusion.3
  200.0 0.2 convolution_multiply_fusion.4
  200.2 0.2 convolution_multiply_fusion.5
  200.4 0.2 convolution_multiply_fusion.6
  200.6 0.2 convolution_multiply_fusion
  200.8 0.2 fusion.22
  201.0 12.5 %all_to_all.21 = bf16[2,8,1024]{2,0,1:T(2,128)(2,1)S(1)} all-to-all(bf16[2,8,1024]{2,0,1:T(2,128)(2,1)S(1)} %copy.35), channel_id=1, replica_groups=mesh['energy'=8,'section'=4] {'energy'}, dimensions={1} | all-to-all | bytes 65536 | tf_op jit(solution)/shard_map/all_to_all | solution.py:148
  213.5 0.7 copy.36
  (27 shorter events, 0.5 us)
Async XLA Ops:
  3.8 16.9 %copy-start = (bf16[1,1,2,384,384]{4,3,2,1,0:T(8,128)(2,1)S(1)}, bf16[1,1,2,384,384]{4,3,2,1,0:T(8,128)(2,1)}, u32[]{:S(2)}) copy-start(bf16[1,1,2,384,384]{4,3,2,1,0:T(8,128)(2,1)} %param.13) | copy-start | bytes 1769476
  4.2 3.2 %collective-permute-start.1 = (bf16[1,384,128]{1,2,0:T(8,128)(2,1)S(1)}, bf16[1,384,128]{1,2,0:T(8,128)(2,1)S(1)}, u32[]{:S(2)}, u32[]{:S(2)}) collective-permute-start(bf16[1,384,128]{1,2,0:T(8,128)(2,1)S(1)} %fusion.94), channel_id=1, source_target_pairs={{1,0},{2,1},{3,2},{5,4},{6,5},{7,6},{9,8},{10,9},{11,10},{13,12},{... | collective-permute-start | bytes 294920 | tf_op jit(solution)/shard_map/while/body/eval_jaxpr/ppermute | solution.py:10
  7.7 6.8 %collective-permute-start.1 = (bf16[1,384,128]{1,2,0:T(8,128)(2,1)S(1)}, bf16[1,384,128]{1,2,0:T(8,128)(2,1)S(1)}, u32[]{:S(2)}, u32[]{:S(2)}) collective-permute-start(bf16[1,384,128]{1,2,0:T(8,128)(2,1)S(1)} %fusion.94), channel_id=1, source_target_pairs={{1,0},{2,1},{3,2},{5,4},{6,5},{7,6},{9,8},{10,9},{11,10},{13,12},{... | collective-permute-start | bytes 294920 | tf_op jit(solution)/shard_map/while/body/eval_jaxpr/ppermute | solution.py:10
  14.8 5.9 %collective-permute-start.1 = (bf16[1,384,128]{1,2,0:T(8,128)(2,1)S(1)}, bf16[1,384,128]{1,2,0:T(8,128)(2,1)S(1)}, u32[]{:S(2)}, u32[]{:S(2)}) collective-permute-start(bf16[1,384,128]{1,2,0:T(8,128)(2,1)S(1)} %fusion.94), channel_id=1, source_target_pairs={{1,0},{2,1},{3,2},{5,4},{6,5},{7,6},{9,8},{10,9},{11,10},{13,12},{... | collective-permute-start | bytes 294920 | tf_op jit(solution)/shard_map/while/body/eval_jaxpr/ppermute | solution.py:10
  20.7 0.9 copy-start.1
  22.2 6.1 %collective-permute-start = (bf16[1,384,128]{1,2,0:T(8,128)(2,1)S(1)}, bf16[1,384,128]{1,2,0:T(8,128)(2,1)S(1)}, u32[]{:S(2)}, u32[]{:S(2)}) collective-permute-start(bf16[1,384,128]{1,2,0:T(8,128)(2,1)S(1)} %fusion.90), channel_id=1, source_target_pairs={{0,1},{1,2},{2,3},{4,5},{5,6},{6,7},{8,9},{9,10},{10,11},{12,13},{... | collective-permute-start | bytes 294920 | tf_op jit(solution)/shard_map/while/body/eval_jaxpr/ppermute | solution.py:10
  28.6 3.5 %collective-permute-start = (bf16[1,384,128]{1,2,0:T(8,128)(2,1)S(1)}, bf16[1,384,128]{1,2,0:T(8,128)(2,1)S(1)}, u32[]{:S(2)}, u32[]{:S(2)}) collective-permute-start(bf16[1,384,128]{1,2,0:T(8,128)(2,1)S(1)} %fusion.90), channel_id=1, source_target_pairs={{0,1},{1,2},{2,3},{4,5},{5,6},{6,7},{8,9},{9,10},{10,11},{12,13},{... | collective-permute-start | bytes 294920 | tf_op jit(solution)/shard_map/while/body/eval_jaxpr/ppermute | solution.py:10
  32.6 5.9 %collective-permute-start = (bf16[1,384,128]{1,2,0:T(8,128)(2,1)S(1)}, bf16[1,384,128]{1,2,0:T(8,128)(2,1)S(1)}, u32[]{:S(2)}, u32[]{:S(2)}) collective-permute-start(bf16[1,384,128]{1,2,0:T(8,128)(2,1)S(1)} %fusion.90), channel_id=1, source_target_pairs={{0,1},{1,2},{2,3},{4,5},{5,6},{6,7},{8,9},{9,10},{10,11},{12,13},{... | collective-permute-start | bytes 294920 | tf_op jit(solution)/shard_map/while/body/eval_jaxpr/ppermute | solution.py:10
  168.4 9.7 %copy-start.2 = (s32[8]{0:T(128)S(1)}, s32[8]{0:T(128)}, u32[]{:S(2)}) copy-start(s32[8]{0:T(128)} %param.18) | copy-start | bytes 100
  172.3 12.8 %all-to-all-start = ((bf16[8,2,1024]{2,1,0:T(2,128)(2,1)}), bf16[8,2,1024]{2,1,0:T(2,128)(2,1)S(1)}, u32[]{:S(2)}, u32[]{:S(2)}) async-start(bf16[8,2,1024]{2,1,0:T(2,128)(2,1)} %reshape.584), calls=%async_computation | async-start | bytes 65536 | tf_op jit(solution)/shard_map/all_to_all | solution.py:138
where the time goes:
time: 218 us; the launch traced here: 214 us
  local copies, waits for them, and re-layouts  89.8 us (41%)
  other arithmetic  70.3 us (32%)
  starting transfers between devices  22.5 us (10%)
  waiting for transfers between devices  14.8 us (7%)
  blocking collectives  12.5 us (6%)
  matrix products  3.87 us (2%)
    unnamed x1, other arithmetic  45.4 us
    gather x1, local copies, waits for them, and re-layouts, lesser(): right_rows = jnp.take(adjoint_rows, right_index, axis=0)  29.4 us
    gather x1, local copies, waits for them, and re-layouts, lesser(): left_rows = jnp.take(field_rows, left_index, axis=0)  29.4 us
    ppermute x6, starting transfers between devices, passed_along(): lax.ppermute(value, axis, [(source, source + steps) for source in range(l...  16.6 us
    ppermute x6, waiting for transfers between devices, passed_along(): lax.ppermute(value, axis, [(source, source + steps) for source in range(l...  14.8 us
    all_to_all x1, blocking collectives, on_device(): lax.all_to_all(as_sent(block_result), 'energy', split_axis=1, concat_axis...  12.5 us
    unnamed x11, local copies, waits for them, and re-layouts  12.2 us
    all_to_all x1, local copies, waits for them, and re-layouts, on_device(): lax.all_to_all(as_sent(lesser_part), 'energy', split_axis=2, concat_axis=...  8.07 us
  transfers between devices with their start and end apart: 7, of which 6 were waited for; matrix products, arithmetic and copies ran while one was open for 3% of the time, Pallas kernels for 0%

commit v1 on v0

v1 whole, which is shorter than its diff:
```python
import functools
import jax
import jax.numpy as jnp
from jax import lax
from jax.experimental import pallas as pl
from jax.experimental.pallas import tpu as pltpu
from jax.sharding import PartitionSpec as P

MESH = pl.DeviceIdType.MESH
F32 = jnp.float32
BF16 = jnp.bfloat16
LANES = 128
FOLD = 64
REACH = 6


def sweep_kernel(
    energies, sections,
    prop_hbm, fsrc_hbm, bsrc_hbm, left_hbm, right_hbm, shift_ref, coup_hbm,
    out_ref,
    prop, fsrc, bsrc, left, right, coup,
    bsrc_t, chosen, weight,
    y, w_t, y_in, w_in,
    table, parts, sent, held, totals, gathered,
    load_sems, fwd_send, fwd_recv, bwd_send, bwd_recv,
    send_one, recv_one, send_two, recv_two,
):
    me = lax.axis_index("energy")
    s = lax.axis_index("section")
    orb = prop.shape[1]
    cols = y.shape[1]
    half = cols // 2
    block = chosen.shape[2]
    rows = block // LANES

    barrier = pltpu.get_barrier_semaphore()
    for j in range(1, energies):
        pl.semaphore_signal(
            barrier, inc=1, device_id={"energy": lax.rem(me + j, energies)}, device_id_type=MESH
        )

    @pl.when(s > 0)
    def _():
        pl.semaphore_signal(barrier, inc=1, device_id={"section": s - 1}, device_id_type=MESH)

    @pl.when(s < sections - 1)
    def _():
        pl.semaphore_signal(barrier, inc=1, device_id={"section": s + 1}, device_id_type=MESH)

    own = pl.ds(pl.multiple_of(me * block, LANES), block)
    loads = [
        pltpu.make_async_copy(fsrc_hbm, fsrc, load_sems.at[0]),
        pltpu.make_async_copy(bsrc_hbm, bsrc, load_sems.at[1]),
        pltpu.make_async_copy(left_hbm, left, load_sems.at[2]),
        pltpu.make_async_copy(right_hbm, right, load_sems.at[3]),
        pltpu.make_async_copy(prop_hbm, prop, load_sems.at[4]),
        pltpu.make_async_copy(coup_hbm.at[:, own], coup, load_sems.at[5]),
    ]
    for load in loads:
        load.start()

    zeros = jnp.zeros((REACH,) + held.shape[1:], held.dtype)
    held[pl.ds(0, REACH)] = zeros
    held[pl.ds(REACH + energies, REACH)] = zeros

    fwd = pltpu.make_async_remote_copy(
        src_ref=y, dst_ref=y_in, send_sem=fwd_send, recv_sem=fwd_recv,
        device_id={"section": lax.rem(s + 1, sections)}, device_id_type=MESH,
    )
    bwd = pltpu.make_async_remote_copy(
        src_ref=w_t, dst_ref=w_in, send_sem=bwd_send, recv_sem=bwd_recv,
        device_id={"section": lax.rem(s + sections - 1, sections)}, device_id_type=MESH,
    )

    loads[1].wait()
    bsrc_t[...] = bsrc[...].astype(F32).T
    for at in (0, 2, 3, 4, 5):
        loads[at].wait()
    base = s * orb

    def choose(b, carry):
        spot = lax.broadcasted_iota(jnp.int32, (orb, LANES), 0)
        for i in range(rows):
            row = left[pl.ds(b * rows + i, 1), :] - base
            chosen[b, :, i * LANES:(i + 1) * LANES] = jnp.where(spot == row, 1.0, 0.0).astype(BF16)
        return carry

    greeted = (energies - 1) + (s > 0).astype(jnp.int32) + (s < sections - 1).astype(jnp.int32)
    pl.semaphore_wait(barrier, greeted)

    def turn(t, carry):
        @pl.when(s == t)
        def _():
            @pl.when(s == 0)
            def _():
                y[...] = fsrc[...]

            @pl.when(s > 0)
            def _():
                fwd.wait_recv()
                current = y_in[...]
                first = jnp.dot(prop[0], current, preferred_element_type=F32)
                second = jnp.dot(prop[1], current, preferred_element_type=F32)
                lane = lax.broadcasted_iota(jnp.int32, second.shape, 1)
                crossed = pltpu.roll(second, half, 1)
                crossed = jnp.where(lane < half, -crossed, crossed)
                y[...] = (first + crossed + fsrc[...].astype(F32)).astype(BF16)

            @pl.when(s < sections - 1)
            def _():
                fwd.start()

        @pl.when(s == sections - 1 - t)
        def _():
            @pl.when(s == sections - 1)
            def _():
                w_t[...] = bsrc_t[...].astype(BF16)

            @pl.when(s < sections - 1)
            def _():
                bwd.wait_recv()
                current = w_in[...]
                first = jnp.dot(current, prop[0], preferred_element_type=F32)
                second = jnp.dot(current, prop[1], preferred_element_type=F32)
                crossed = jnp.concatenate([second[half:], -second[:half]], axis=0)
                w_t[...] = (first + crossed + bsrc_t[...]).astype(BF16)

            @pl.when(s > 0)
            def _():
                bwd.start()

        @pl.when(t < sections - 1)
        def _():
            lax.fori_loop(
                t * energies // (sections - 1), (t + 1) * energies // (sections - 1), choose, 0
            )

        return carry

    lax.fori_loop(0, sections, turn, 0)

    scale = half ** (-0.5)
    ahead = y[...]
    wide = ahead.astype(F32)
    lane = lax.broadcasted_iota(jnp.int32, wide.shape, 1)
    turned = pltpu.roll(wide, half, 1)
    turned = jnp.where(lane < half, turned, -turned).astype(BF16)
    behind = w_t[...].astype(F32).T.astype(BF16)
    both = (((1,), (1,)), ((), ()))
    for member, operand in enumerate((ahead, turned)):
        product = lax.dot_general(behind, operand, both, preferred_element_type=F32)
        for tile in range(orb // LANES):
            folded = None
            for q in range(max(0, tile * 2 - 1), min(orb // FOLD, tile * 2 + 3)):
                piece = product[q * FOLD:(q + 1) * FOLD, tile * LANES:(tile + 1) * LANES]
                right_at = q * FOLD + lax.broadcasted_iota(jnp.int32, piece.shape, 0)
                left_at = tile * LANES + lax.broadcasted_iota(jnp.int32, piece.shape, 1)
                kept = jnp.where(jnp.abs(right_at - left_at) < FOLD // 2, piece, 0.0)
                folded = kept if folded is None else folded + kept
            table[member * FOLD:(member + 1) * FOLD, tile * LANES:(tile + 1) * LANES] = (
                folded * scale
            ).astype(BF16)

    def exchange_one(other):
        return pltpu.make_async_remote_copy(
            src_ref=sent.at[other], dst_ref=held.at[REACH + me],
            send_sem=send_one.at[other], recv_sem=recv_one.at[me],
            device_id={"energy": other}, device_id_type=MESH,
        )

    def exchange_two(other):
        return pltpu.make_async_remote_copy(
            src_ref=totals.at[other], dst_ref=gathered.at[me],
            send_sem=send_two.at[other], recv_sem=recv_two.at[me],
            device_id={"energy": other}, device_id_type=MESH,
        )

    def arrived(other, sems, buffer, at):
        return pltpu.make_async_remote_copy(
            src_ref=buffer.at[at], dst_ref=buffer.at[at],
            send_sem=sems.at[other], recv_sem=sems.at[other],
            device_id={"energy": other}, device_id_type=MESH,
        )

    def pick(b):
        spread = jnp.dot(table[...], chosen[b], preferred_element_type=F32)
        for i in range(rows):
            row = (right[pl.ds(b * rows + i, 1), :] - base) & (FOLD - 1)
            spot = lax.broadcasted_iota(jnp.int32, (FOLD, LANES), 0) == row
            for member in range(2):
                piece = spread[member * FOLD:(member + 1) * FOLD, i * LANES:(i + 1) * LANES]
                parts[pl.ds(member * rows + i, 1), :] = jnp.sum(
                    jnp.where(spot, piece, 0.0), axis=0, keepdims=True
                )
        return parts[...].astype(BF16)

    def serve(j, carry):
        other = lax.rem(me + j, energies)
        sent[other] = pick(other)
        exchange_one(other).start()
        return carry

    lax.fori_loop(1, energies, serve, 0)
    held[REACH + me] = pick(me)

    for k in range(coup.shape[0]):
        for i in range(rows):
            line = coup[k:k + 1, i * LANES:(i + 1) * LANES]
            weight[k, i:i + 1, :] = line
            weight[k, rows + i:rows + i + 1, :] = line

    def await_one(j, carry):
        other = lax.rem(me + j, energies)
        arrived(other, recv_one, held, REACH + other).wait_recv()
        return carry

    lax.fori_loop(1, energies, await_one, 0)

    total = None
    for k in range(coup.shape[0]):
        moved = held[pl.ds(REACH - shift_ref[k], energies)].astype(F32)
        term = weight[k][None] * moved
        total = term if total is None else total + term
    totals[...] = total.astype(BF16)

    def send_back(j, carry):
        exchange_two(lax.rem(me + j, energies)).start()
        return carry

    lax.fori_loop(1, energies, send_back, 0)
    gathered[me] = totals[me]

    def await_two(j, carry):
        other = lax.rem(me + j, energies)
        arrived(other, recv_two, gathered, other).wait_recv()
        return carry

    lax.fori_loop(1, energies, await_two, 0)
    for b in range(energies):
        for member in range(2):
            out_ref[member, b * rows:(b + 1) * rows, :] = gathered[
                b, member * rows:(member + 1) * rows, :
            ].astype(F32)

    def settle(j, carry):
        other = lax.rem(me + j, energies)
        exchange_one(other).wait_send()
        exchange_two(other).wait_send()
        return carry

    lax.fori_loop(1, energies, settle, 0)

    @pl.when(s < sections - 1)
    def _():
        fwd.wait_send()

    @pl.when(s > 0)
    def _():
        bwd.wait_send()


def on_device(
    propagator, forward_source, backward_source, left_orbital, right_orbital, phonon_shift, coupling
):
    energies = lax.axis_size("energy")
    sections = lax.axis_size("section")
    orb = propagator.shape[3]
    cols = forward_source.shape[3]
    pairs = left_orbital.shape[0]
    phonons = coupling.shape[0]
    block = pairs // energies
    rows = block // LANES
    tall = max(16, 2 * rows)
    anywhere = pl.BlockSpec(memory_space=pl.ANY)
    out = pl.pallas_call(
        functools.partial(sweep_kernel, energies, sections),
        out_shape=jax.ShapeDtypeStruct((2, pairs // LANES, LANES), F32),
        in_specs=[anywhere] * 5 + [pl.BlockSpec(memory_space=pltpu.SMEM), anywhere],
        out_specs=pl.BlockSpec(memory_space=pltpu.VMEM),
        scratch_shapes=[
            pltpu.VMEM((2, orb, orb), BF16),
            pltpu.VMEM((orb, cols), BF16),
            pltpu.VMEM((orb, cols), BF16),
            pltpu.VMEM((pairs // LANES, LANES), jnp.int32),
            pltpu.VMEM((pairs // LANES, LANES), jnp.int32),
            pltpu.VMEM((phonons, block), F32),
            pltpu.VMEM((cols, orb), F32),
            pltpu.VMEM((energies, orb, block), BF16),
            pltpu.VMEM((phonons, tall, LANES), F32),
            pltpu.VMEM((orb, cols), BF16),
            pltpu.VMEM((cols, orb), BF16),
            pltpu.VMEM((orb, cols), BF16),
            pltpu.VMEM((cols, orb), BF16),
            pltpu.VMEM((2 * FOLD, orb), BF16),
            pltpu.VMEM((tall, LANES), F32),
            pltpu.VMEM((energies, tall, LANES), BF16),
            pltpu.VMEM((energies + 2 * REACH, tall, LANES), BF16),
            pltpu.VMEM((energies, tall, LANES), BF16),
            pltpu.VMEM((energies, tall, LANES), BF16),
            pltpu.SemaphoreType.DMA((6,)),
            pltpu.SemaphoreType.DMA,
            pltpu.SemaphoreType.DMA,
            pltpu.SemaphoreType.DMA,
            pltpu.SemaphoreType.DMA,
            pltpu.SemaphoreType.DMA((energies,)),
            pltpu.SemaphoreType.DMA((energies,)),
            pltpu.SemaphoreType.DMA((energies,)),
            pltpu.SemaphoreType.DMA((energies,)),
        ],
        compiler_params=pltpu.CompilerParams(
            collective_id=0, has_side_effects=True, vmem_limit_bytes=40 * 2**20
        ),
    )(
        propagator.reshape(2, orb, orb),
        forward_source.reshape(orb, cols),
        backward_source.reshape(orb, cols),
        left_orbital.reshape(pairs // LANES, LANES),
        right_orbital.reshape(pairs // LANES, LANES),
        phonon_shift,
        coupling,
    )
    return out.reshape(2, 1, pairs)


def solution(mesh):
    placed = (
        P("energy", "section", None, None, None),
        P("energy", "section", None, None),
        P("energy", "section", None, None),
        P("section"),
        P("section"),
        P(),
        P(None, "section"),
    )
    return jax.shard_map(
        on_device,
        mesh=mesh,
        in_specs=placed,
        out_specs=P(None, "energy", "section"),
        check_vma=False,
    )
```

time: 218 us -> 30.7 us (0.14); the launches traced: 214 us -> 30.3 us
  local copies, waits for them, and re-layouts: 89.8 us -> 6.6 us
  other arithmetic: 70.3 us -> 0 us
  Pallas kernels: 0 us -> 23.7 us
  starting transfers between devices: 22.5 us -> 0 us
  waiting for transfers between devices: 14.8 us -> 0 us
  blocking collectives: 12.5 us -> 0 us
  matrix products: 3.87 us -> 0 us
    gather x2 -> x0, local copies, waits for them, and re-layouts: 58.8 us -> none  [the longest x1 29.4 us: lesser(): right_rows = jnp.take(adjoint_rows, right_index, axis=0)]
    unnamed x1 -> x0, other arithmetic: 45.4 us -> none
    pallas_call x0 -> x1, Pallas kernels: none -> 23.7 us  [on_device(): pl.pallas_call(functools.partial(sweep_kernel, energies, sections), out_s...]
    ppermute x6 -> x0, starting transfers between devices: 16.6 us -> none  [passed_along(): lax.ppermute(value, axis, [(source, source + steps) for source in range(l...]
    ppermute x6 -> x0, waiting for transfers between devices: 14.8 us -> none  [passed_along(): lax.ppermute(value, axis, [(source, source + steps) for source in range(l...]
    all_to_all x1 -> x0, blocking collectives: 12.5 us -> none  [on_device(): lax.all_to_all(as_sent(block_result), 'energy', split_axis=1, concat_axis...]
    select_n x2 -> x0, other arithmetic: 11.6 us -> none  [the longest x1 5.82 us: lesser(): right_rows = jnp.take(adjoint_rows, right_index, axis=0)]
    all_to_all x1 -> x0, local copies, waits for them, and re-layouts: 8.07 us -> none  [on_device(): lax.all_to_all(as_sent(lesser_part), 'energy', split_axis=2, concat_axis=...]
  transfers between devices with their start and end apart: 7 -> 0, of which waited for: 6 -> 0; matrix products, arithmetic and copies ran while one was open for 3% -> 0% of each run, Pallas kernels for 0% -> 0%
where the time goes in v1:
time: 30.7 us; the launch traced here: 30.3 us
  Pallas kernels  23.7 us (77%)
  local copies, waits for them, and re-layouts  6.6 us (21%)
    pallas_call x1, Pallas kernels, on_device(): pl.pallas_call(functools.partial(sweep_kernel, energies, sections), out_s...  23.7 us
    unnamed x15, local copies, waits for them, and re-layouts  6.6 us

profile of v1, /device:TPU:0, one launch (start us, length us, event | category | flops | bytes accessed | tf_op | source)
XLA Modules:
  0.0 30.3 jit_solution(9324881530142231858)
XLA Ops:
  0.0 0.0 copy-start.6
  0.0 0.7 %copy-done.6 = s32[8]{0:T(128)S(1)} copy-done((s32[8]{0:T(128)S(1)}, s32[8]{0:T(128)}, u32[]{:S(2)}) %copy-start.6) | copy-done | bytes 56
  0.7 0.0 copy-start
  0.7 1.1 %copy-done = bf16[1,1,2,384,384]{4,3,2,1,0:T(8,128)(2,1)S(1)} copy-done((bf16[1,1,2,384,384]{4,3,2,1,0:T(8,128)(2,1)S(1)}, bf16[1,1,2,384,384]{4,3,2,1,0:T(8,128)(2,1)}, u32[]{:S(2)}) %copy-start) | copy-done | bytes 589848
  1.7 0.0 copy-start.1
  1.7 0.9 %copy-done.1 = f32[8,8192]{1,0:T(8,128)S(1)} copy-done((f32[8,8192]{1,0:T(8,128)S(1)}, f32[8,8192]{1,0:T(8,128)}, u32[]{:S(2)}) %copy-start.1) | copy-done | bytes 262168
  2.7 0.0 copy-start.2
  2.7 0.9 %copy-done.2 = bf16[1,1,384,128]{3,2,1,0:T(8,128)(2,1)S(1)} copy-done((bf16[1,1,384,128]{3,2,1,0:T(8,128)(2,1)S(1)}, bf16[1,1,384,128]{3,2,1,0:T(8,128)(2,1)}, u32[]{:S(2)}) %copy-start.2) | copy-done | bytes 98328
  3.6 0.0 copy-start.3
  3.6 0.9 %copy-done.3 = bf16[1,1,384,128]{3,2,1,0:T(8,128)(2,1)S(1)} copy-done((bf16[1,1,384,128]{3,2,1,0:T(8,128)(2,1)S(1)}, bf16[1,1,384,128]{3,2,1,0:T(8,128)(2,1)}, u32[]{:S(2)}) %copy-start.3) | copy-done | bytes 98328
  4.5 0.0 copy-start.4
  4.5 0.8 %copy-done.4 = s32[8192]{0:T(1024)S(1)} copy-done((s32[8192]{0:T(1024)S(1)}, s32[8192]{0:T(1024)}, u32[]{:S(2)}) %copy-start.4) | copy-done | bytes 32792
  5.2 0.0 copy-start.5
  5.2 0.8 %copy-done.5 = s32[8192]{0:T(1024)S(1)} copy-done((s32[8192]{0:T(1024)S(1)}, s32[8192]{0:T(1024)}, u32[]{:S(2)}) %copy-start.5) | copy-done | bytes 32792
  6.0 23.7 %shard_map.73 = f32[2,64,128]{2,1,0:T(8,128)S(1)} custom-call(bf16[2,384,384]{2,1,0:T(8,128)(2,1)S(1)} %bitcast.6, bf16[384,128]{1,0:T(8,128)(2,1)S(1)} %bitcast.8, bf16[384,128]{1,0:T(8,128)(2,1)S(1)} %bitcast.9, s32[64,128]{1,0:T(8,128)S(1)} %bitcast.10, s32[64,128]{1,0:T(8,128)S(1)} %bitcast.11, s32[8]{0:T(128)S(1)} %copy-done.6, f32[8,8192]{1,0:T(8,128)S(1)} %copy-done.1), custom_call_target="tpu_custom_call" | custom-call | tf_op jit(solution)/shard_map/pallas_call | solution.py:275
  29.6 0.6 %copy.10 = f32[2,1,8192]{2,1,0:T(1,128)} copy(f32[2,1,8192]{2,1,0:T(1,128)S(1)} %bitcast.7) | data formatting | bytes 131072
Async XLA Ops:
  0.0 0.7 %copy-start.6 = (s32[8]{0:T(128)S(1)}, s32[8]{0:T(128)}, u32[]{:S(2)}) copy-start(s32[8]{0:T(128)} %shift_ref.1) | copy-start | bytes 100
  0.7 1.1 %copy-start = (bf16[1,1,2,384,384]{4,3,2,1,0:T(8,128)(2,1)S(1)}, bf16[1,1,2,384,384]{4,3,2,1,0:T(8,128)(2,1)}, u32[]{:S(2)}) copy-start(bf16[1,1,2,384,384]{4,3,2,1,0:T(8,128)(2,1)} %param.7) | copy-start | bytes 1769476
  1.7 0.9 %copy-start.1 = (f32[8,8192]{1,0:T(8,128)S(1)}, f32[8,8192]{1,0:T(8,128)}, u32[]{:S(2)}) copy-start(f32[8,8192]{1,0:T(8,128)} %coup_hbm.1) | copy-start | bytes 786436
  2.7 0.9 %copy-start.2 = (bf16[1,1,384,128]{3,2,1,0:T(8,128)(2,1)S(1)}, bf16[1,1,384,128]{3,2,1,0:T(8,128)(2,1)}, u32[]{:S(2)}) copy-start(bf16[1,1,384,128]{3,2,1,0:T(8,128)(2,1)} %param.8) | copy-start | bytes 294916
  3.6 0.9 %copy-start.3 = (bf16[1,1,384,128]{3,2,1,0:T(8,128)(2,1)S(1)}, bf16[1,1,384,128]{3,2,1,0:T(8,128)(2,1)}, u32[]{:S(2)}) copy-start(bf16[1,1,384,128]{3,2,1,0:T(8,128)(2,1)} %param.9) | copy-start | bytes 294916
  4.5 0.8 %copy-start.4 = (s32[8192]{0:T(1024)S(1)}, s32[8192]{0:T(1024)}, u32[]{:S(2)}) copy-start(s32[8192]{0:T(1024)} %param.10) | copy-start | bytes 98308
  5.2 0.8 %copy-start.5 = (s32[8192]{0:T(1024)S(1)}, s32[8192]{0:T(1024)}, u32[]{:S(2)}) copy-start(s32[8192]{0:T(1024)} %param.11) | copy-start | bytes 98308

commit v2 on v1

--- a/solution.py
+++ b/solution.py
@@ -20,9 +20,9 @@
     out_ref,
     prop, fsrc, bsrc, left, right, coup,
     bsrc_t, chosen, weight,
-    y, w_t, y_in, w_in,
+    y, w_t, y_in, w_in, w_end,
     table, parts, sent, held, totals, gathered,
-    load_sems, fwd_send, fwd_recv, bwd_send, bwd_recv,
+    load_sems, fwd_send, fwd_recv, bwd_send, bwd_recv, end_send, end_recv,
     send_one, recv_one, send_two, recv_two,
 ):
     me = lax.axis_index("energy")
@@ -63,19 +63,18 @@
     held[pl.ds(0, REACH)] = zeros
     held[pl.ds(REACH + energies, REACH)] = zeros
 
-    fwd = pltpu.make_async_remote_copy(
-        src_ref=y, dst_ref=y_in, send_sem=fwd_send, recv_sem=fwd_recv,
-        device_id={"section": lax.rem(s + 1, sections)}, device_id_type=MESH,
-    )
-    bwd = pltpu.make_async_remote_copy(
-        src_ref=w_t, dst_ref=w_in, send_sem=bwd_send, recv_sem=bwd_recv,
-        device_id={"section": lax.rem(s + sections - 1, sections)}, device_id_type=MESH,
-    )
-
-    loads[1].wait()
-    bsrc_t[...] = bsrc[...].astype(F32).T
-    for at in (0, 2, 3, 4, 5):
-        loads[at].wait()
+    after, before = lax.rem(s + 1, sections), lax.rem(s + sections - 1, sections)
+
+    def passed(source, target, send_sem, recv_sem, to):
+        return pltpu.make_async_remote_copy(
+            src_ref=source, dst_ref=target, send_sem=send_sem, recv_sem=recv_sem,
+            device_id={"section": to}, device_id_type=MESH,
+        )
+
+    fwd_first = passed(fsrc_hbm, y_in, fwd_send, fwd_recv, after)
+    fwd = passed(y, y_in, fwd_send, fwd_recv, after)
+    bwd_first = passed(bsrc_hbm, w_end, end_send, end_recv, before)
+    bwd = passed(w_t, w_in, bwd_send, bwd_recv, before)
     base = s * orb
 
     def choose(b, carry):
@@ -88,23 +87,45 @@
     greeted = (energies - 1) + (s > 0).astype(jnp.int32) + (s < sections - 1).astype(jnp.int32)
     pl.semaphore_wait(barrier, greeted)
 
+    @pl.when(s == 0)
+    def _():
+        fwd_first.start()
+
+    @pl.when(s == sections - 1)
+    def _():
+        bwd_first.start()
+
+    for at in (0, 1, 2):
+        loads[at].wait()
+    bsrc_t[...] = bsrc[...].astype(F32).T
+
+    @pl.when(s == 0)
+    def _():
+        y[...] = fsrc[...]
+
+    @pl.when(s == sections - 1)
+    def _():
+        w_t[...] = bsrc_t[...].astype(BF16)
+
+    def build(t):
+        lax.fori_loop(
+            t * energies // (sections - 1), (t + 1) * energies // (sections - 1), choose, 0
+        )
+
+    build(0)
+    loads[4].wait()
+
     def turn(t, carry):
         @pl.when(s == t)
         def _():
-            @pl.when(s == 0)
-            def _():
-                y[...] = fsrc[...]
-
-            @pl.when(s > 0)
-            def _():
-                fwd.wait_recv()
-                current = y_in[...]
-                first = jnp.dot(prop[0], current, preferred_element_type=F32)
-                second = jnp.dot(prop[1], current, preferred_element_type=F32)
-                lane = lax.broadcasted_iota(jnp.int32, second.shape, 1)
-                crossed = pltpu.roll(second, half, 1)
-                crossed = jnp.where(lane < half, -crossed, crossed)
-                y[...] = (first + crossed + fsrc[...].astype(F32)).astype(BF16)
+            fwd.wait_recv()
+            current = y_in[...]
+            first = jnp.dot(prop[0], current, preferred_element_type=F32)
+            second = jnp.dot(prop[1], current, preferred_element_type=F32)
+            lane = lax.broadcasted_iota(jnp.int32, second.shape, 1)
+            crossed = pltpu.roll(second, half, 1)
+            crossed = jnp.where(lane < half, -crossed, crossed)
+            y[...] = (first + crossed + fsrc[...].astype(F32)).astype(BF16)
 
             @pl.when(s < sections - 1)
             def _():
@@ -112,18 +133,20 @@
 
         @pl.when(s == sections - 1 - t)
         def _():
-            @pl.when(s == sections - 1)
+            @pl.when(t == 1)
             def _():
-                w_t[...] = bsrc_t[...].astype(BF16)
-
-            @pl.when(s < sections - 1)
+                bwd_first.wait_recv()
+                w_in[...] = w_end[...].astype(F32).T.astype(BF16)
+
+            @pl.when(t > 1)
             def _():
                 bwd.wait_recv()
-                current = w_in[...]
-                first = jnp.dot(current, prop[0], preferred_element_type=F32)
-                second = jnp.dot(current, prop[1], preferred_element_type=F32)
-                crossed = jnp.concatenate([second[half:], -second[:half]], axis=0)
-                w_t[...] = (first + crossed + bsrc_t[...]).astype(BF16)
+
+            current = w_in[...]
+            first = jnp.dot(current, prop[0], preferred_element_type=F32)
+            second = jnp.dot(current, prop[1], preferred_element_type=F32)
+            crossed = jnp.concatenate([second[half:], -second[:half]], axis=0)
+            w_t[...] = (first + crossed + bsrc_t[...]).astype(BF16)
 
             @pl.when(s > 0)
             def _():
@@ -131,13 +154,19 @@
 
         @pl.when(t < sections - 1)
         def _():
-            lax.fori_loop(
-                t * energies // (sections - 1), (t + 1) * energies // (sections - 1), choose, 0
-            )
-
-        return carry
-
-    lax.fori_loop(0, sections, turn, 0)
+            build(t)
+
+        return carry
+
+    lax.fori_loop(1, sections, turn, 0)
+    loads[3].wait()
+    loads[5].wait()
+
+    for k in range(coup.shape[0]):
+        for i in range(rows):
+            line = coup[k:k + 1, i * LANES:(i + 1) * LANES]
+            weight[k, i:i + 1, :] = line
+            weight[k, rows + i:rows + i + 1, :] = line
 
     scale = half ** (-0.5)
     ahead = y[...]
@@ -203,12 +232,6 @@
     lax.fori_loop(1, energies, serve, 0)
     held[REACH + me] = pick(me)
 
-    for k in range(coup.shape[0]):
-        for i in range(rows):
-            line = coup[k:k + 1, i * LANES:(i + 1) * LANES]
-            weight[k, i:i + 1, :] = line
-            weight[k, rows + i:rows + i + 1, :] = line
-
     def await_one(j, carry):
         other = lax.rem(me + j, energies)
         arrived(other, recv_one, held, REACH + other).wait_recv()
@@ -254,7 +277,11 @@
     def _():
         fwd.wait_send()
 
-    @pl.when(s > 0)
+    @pl.when(s == sections - 1)
+    def _():
+        bwd_first.wait_send()
+
+    @pl.when((s > 0) & (s < sections - 1))
     def _():
         bwd.wait_send()
 
@@ -271,11 +298,11 @@
     block = pairs // energies
     rows = block // LANES
     tall = max(16, 2 * rows)
-    anywhere = pl.BlockSpec(memory_space=pl.ANY)
+    in_hbm = pl.BlockSpec(memory_space=pltpu.HBM)
     out = pl.pallas_call(
         functools.partial(sweep_kernel, energies, sections),
         out_shape=jax.ShapeDtypeStruct((2, pairs // LANES, LANES), F32),
-        in_specs=[anywhere] * 5 + [pl.BlockSpec(memory_space=pltpu.SMEM), anywhere],
+        in_specs=[in_hbm] * 5 + [pl.BlockSpec(memory_space=pltpu.SMEM), in_hbm],
         out_specs=pl.BlockSpec(memory_space=pltpu.VMEM),
         scratch_shapes=[
             pltpu.VMEM((2, orb, orb), BF16),
@@ -291,6 +318,7 @@
             pltpu.VMEM((cols, orb), BF16),
             pltpu.VMEM((orb, cols), BF16),
             pltpu.VMEM((cols, orb), BF16),
+            pltpu.VMEM((orb, cols), BF16),
             pltpu.VMEM((2 * FOLD, orb), BF16),
             pltpu.VMEM((tall, LANES), F32),
             pltpu.VMEM((energies, tall, LANES), BF16),
@@ -302,13 +330,15 @@
             pltpu.SemaphoreType.DMA,
             pltpu.SemaphoreType.DMA,
             pltpu.SemaphoreType.DMA,
+            pltpu.SemaphoreType.DMA,
+            pltpu.SemaphoreType.DMA,
             pltpu.SemaphoreType.DMA((energies,)),
             pltpu.SemaphoreType.DMA((energies,)),
             pltpu.SemaphoreType.DMA((energies,)),
             pltpu.SemaphoreType.DMA((energies,)),
         ],
         compiler_params=pltpu.CompilerParams(
-            collective_id=0, has_side_effects=True, vmem_limit_bytes=40 * 2**20
+            collective_id=0, has_side_effects=True, vmem_limit_bytes=63 * 2**20
         ),
     )(
         propagator.reshape(2, orb, orb),

time: 30.7 us -> 26.3 us (0.86)
  local copies, waits for them, and re-layouts: 6.6 us -> 1.47 us
  Pallas kernels: 23.7 us -> 24.6 us
    unnamed x15 -> x1, local copies, waits for them, and re-layouts: 6.6 us -> 1.47 us
    pallas_call x1, Pallas kernels: 23.7 us -> 24.6 us  [on_device(): pl.pallas_call(functools.partial(sweep_kernel, energies, sections), out_s...]
where the time goes in v2:
time: 26.3 us; the launch traced here: 26.1 us
  Pallas kernels  24.6 us (94%)
  local copies, waits for them, and re-layouts  1.47 us (6%)
    pallas_call x1, Pallas kernels, on_device(): pl.pallas_call(functools.partial(sweep_kernel, energies, sections), out_s...  24.6 us
    unnamed x1, local copies, waits for them, and re-layouts  1.47 us

profile of v2, /device:TPU:0, one launch (start us, length us, event | category | flops | bytes accessed | tf_op | source)
XLA Modules:
  0.0 26.1 jit_solution(17971907972710814438)
XLA Ops:
  0.0 24.6 %shard_map.73 = f32[2,64,128]{2,1,0:T(8,128)} custom-call(bf16[2,384,384]{2,1,0:T(8,128)(2,1)} %bitcast.6, bf16[384,128]{1,0:T(8,128)(2,1)} %bitcast.8, bf16[384,128]{1,0:T(8,128)(2,1)} %bitcast.9, s32[64,128]{1,0:T(8,128)} %bitcast.10, s32[64,128]{1,0:T(8,128)} %bitcast.11, s32[8]{0:T(128)} %shift_ref.1, f32[8,8192]{1,0:T(8,128)} %coup_hbm.1), custom_call_target="tpu_custom_call" | custom-call | tf_op jit(solution)/shard_map/pallas_call | solution.py:302
  24.6 1.5 %copy.10 = f32[2,1,8192]{2,1,0:T(1,128)} copy(f32[2,1,8192]{2,1,0:T(1,128)} %bitcast.7) | data formatting | bytes 131072

commit v3 on v2

--- a/solution.py
+++ b/solution.py
@@ -10,6 +10,8 @@
 F32 = jnp.float32
 BF16 = jnp.bfloat16
 LANES = 128
+DEEP = 256
+DEEP_BITS = 8
 FOLD = 64
 REACH = 6
 
@@ -32,6 +34,7 @@
     half = cols // 2
     block = chosen.shape[2]
     rows = block // LANES
+    groups = table.shape[0] // (2 * FOLD)
 
     barrier = pltpu.get_barrier_semaphore()
     for j in range(1, energies):
@@ -59,6 +62,7 @@
     for load in loads:
         load.start()
 
+    table[...] = jnp.zeros(table.shape, table.dtype)
     zeros = jnp.zeros((REACH,) + held.shape[1:], held.dtype)
     held[pl.ds(0, REACH)] = zeros
     held[pl.ds(REACH + energies, REACH)] = zeros
@@ -78,9 +82,9 @@
     base = s * orb
 
     def choose(b, carry):
-        spot = lax.broadcasted_iota(jnp.int32, (orb, LANES), 0)
+        spot = lax.broadcasted_iota(jnp.int32, (DEEP, LANES), 0)
         for i in range(rows):
-            row = left[pl.ds(b * rows + i, 1), :] - base
+            row = (left[pl.ds(b * rows + i, 1), :] - base) & (DEEP - 1)
             chosen[b, :, i * LANES:(i + 1) * LANES] = jnp.where(spot == row, 1.0, 0.0).astype(BF16)
         return carry
 
@@ -186,9 +190,9 @@
                 left_at = tile * LANES + lax.broadcasted_iota(jnp.int32, piece.shape, 1)
                 kept = jnp.where(jnp.abs(right_at - left_at) < FOLD // 2, piece, 0.0)
                 folded = kept if folded is None else folded + kept
-            table[member * FOLD:(member + 1) * FOLD, tile * LANES:(tile + 1) * LANES] = (
-                folded * scale
-            ).astype(BF16)
+            group, column = tile * LANES // DEEP, tile * LANES % DEEP
+            top = (member * groups + group) * FOLD
+            table[top:top + FOLD, column:column + LANES] = (folded * scale).astype(BF16)
 
     def exchange_one(other):
         return pltpu.make_async_remote_copy(
@@ -211,26 +215,58 @@
             device_id={"energy": other}, device_id_type=MESH,
         )
 
-    def pick(b):
-        spread = jnp.dot(table[...], chosen[b], preferred_element_type=F32)
+    def product_of(b):
+        return jnp.dot(table[...], chosen[b], preferred_element_type=F32)
+
+    def pick(b, spread):
+        eight = (8, LANES)
         for i in range(rows):
-            row = (right[pl.ds(b * rows + i, 1), :] - base) & (FOLD - 1)
-            spot = lax.broadcasted_iota(jnp.int32, (FOLD, LANES), 0) == row
+            right_at = (right[pl.ds(b * rows + i, 1), :] - base) & (FOLD - 1)
+            group = lax.shift_right_logical(left[pl.ds(b * rows + i, 1), :] - base, DEEP_BITS)
+            high = jnp.broadcast_to(
+                group * (FOLD // 8) + lax.shift_right_logical(right_at, 3), eight
+            )
+            low = lax.broadcasted_iota(jnp.int32, eight, 0) == jnp.broadcast_to(right_at & 7, eight)
             for member in range(2):
-                piece = spread[member * FOLD:(member + 1) * FOLD, i * LANES:(i + 1) * LANES]
-                parts[pl.ds(member * rows + i, 1), :] = jnp.sum(
-                    jnp.where(spot, piece, 0.0), axis=0, keepdims=True
+                top = member * groups * FOLD
+                pieces = [
+                    spread[top + 8 * n:top + 8 * n + 8, i * LANES:(i + 1) * LANES]
+                    for n in range(groups * FOLD // 8)
+                ]
+                width = 1 << (len(pieces) - 1).bit_length()
+                while width > 1:
+                    width //= 2
+                    upper = (high & width) != 0
+                    pieces = [
+                        jnp.where(upper, pieces[n + width], piece)
+                        if n + width < len(pieces) else piece
+                        for n, piece in enumerate(pieces[:width])
+                    ]
+                parts[b, pl.ds(member * rows + i, 1), :] = jnp.sum(
+                    jnp.where(low, pieces[0], 0.0), axis=0, keepdims=True
                 )
-        return parts[...].astype(BF16)
-
-    def serve(j, carry):
-        other = lax.rem(me + j, energies)
-        sent[other] = pick(other)
-        exchange_one(other).start()
-        return carry
-
-    lax.fori_loop(1, energies, serve, 0)
-    held[REACH + me] = pick(me)
+        return parts[b].astype(BF16)
+
+    if energies <= 8:
+        spread = product_of(lax.rem(me + 1, energies))
+        for j in range(1, energies + 1):
+            other = lax.rem(me + j, energies)
+            current = spread
+            if j < energies:
+                spread = product_of(lax.rem(me + j + 1, energies))
+                sent[other] = pick(other, current)
+                exchange_one(other).start()
+            else:
+                held[REACH + me] = pick(me, current)
+    else:
+        def serve(j, carry):
+            other = lax.rem(me + j, energies)
+            sent[other] = pick(other, product_of(other))
+            exchange_one(other).start()
+            return carry
+
+        lax.fori_loop(1, energies, serve, 0)
+        held[REACH + me] = pick(me, product_of(me))
 
     def await_one(j, carry):
         other = lax.rem(me + j, energies)
@@ -298,6 +334,7 @@
     block = pairs // energies
     rows = block // LANES
     tall = max(16, 2 * rows)
+    groups = pl.cdiv(orb, DEEP)
     in_hbm = pl.BlockSpec(memory_space=pltpu.HBM)
     out = pl.pallas_call(
         functools.partial(sweep_kernel, energies, sections),
@@ -312,15 +349,15 @@
             pltpu.VMEM((pairs // LANES, LANES), jnp.int32),
             pltpu.VMEM((phonons, block), F32),
             pltpu.VMEM((cols, orb), F32),
-            pltpu.VMEM((energies, orb, block), BF16),
+            pltpu.VMEM((energies, DEEP, block), BF16),
             pltpu.VMEM((phonons, tall, LANES), F32),
             pltpu.VMEM((orb, cols), BF16),
             pltpu.VMEM((cols, orb), BF16),
             pltpu.VMEM((orb, cols), BF16),
             pltpu.VMEM((cols, orb), BF16),
             pltpu.VMEM((orb, cols), BF16),
-            pltpu.VMEM((2 * FOLD, orb), BF16),
-            pltpu.VMEM((tall, LANES), F32),
+            pltpu.VMEM((2 * groups * FOLD, DEEP), BF16),
+            pltpu.VMEM((energies, tall, LANES), F32),
             pltpu.VMEM((energies, tall, LANES), BF16),
             pltpu.VMEM((energies + 2 * REACH, tall, LANES), BF16),
             pltpu.VMEM((energies, tall, LANES), BF16),

time: 26.3 us -> 25.3 us (0.962)
  Pallas kernels: 24.6 us -> 23.7 us
    pallas_call x1, Pallas kernels: 24.6 us -> 23.7 us  [on_device(): pl.pallas_call(functools.partial(sweep_kernel, energies, sections), out_s...]
where the time goes in v3:
time: 25.3 us; the launch traced here: 25.1 us
  Pallas kernels  23.7 us (94%)
  local copies, waits for them, and re-layouts  1.47 us (6%)
    pallas_call x1, Pallas kernels, on_device(): pl.pallas_call(functools.partial(sweep_kernel, energies, sections), out_s...  23.7 us
    unnamed x1, local copies, waits for them, and re-layouts  1.47 us

profile of v3, /device:TPU:0, one launch (start us, length us, event | category | flops | bytes accessed | tf_op | source)
XLA Modules:
  0.0 25.1 jit_solution(6909044102581820368)
XLA Ops:
  0.0 23.7 %shard_map.73 = f32[2,64,128]{2,1,0:T(8,128)} custom-call(bf16[2,384,384]{2,1,0:T(8,128)(2,1)} %bitcast.6, bf16[384,128]{1,0:T(8,128)(2,1)} %bitcast.8, bf16[384,128]{1,0:T(8,128)(2,1)} %bitcast.9, s32[64,128]{1,0:T(8,128)} %bitcast.10, s32[64,128]{1,0:T(8,128)} %bitcast.11, s32[8]{0:T(128)} %shift_ref.1, f32[8,8192]{1,0:T(8,128)} %coup_hbm.1), custom_call_target="tpu_custom_call" | custom-call | tf_op jit(solution)/shard_map/pallas_call | solution.py:339
  23.7 1.5 %copy.10 = f32[2,1,8192]{2,1,0:T(1,128)} copy(f32[2,1,8192]{2,1,0:T(1,128)} %bitcast.7) | data formatting | bytes 131072

commit v4 on v3

--- a/solution.py
+++ b/solution.py
@@ -14,6 +14,18 @@
 DEEP_BITS = 8
 FOLD = 64
 REACH = 6
+
+
+def partner(me, j, count):
+    if count & (count - 1):
+        return lax.rem(me + j, count)
+    found, bit = 0, 1
+    while bit < count:
+        mine = lax.rem(me // bit, 2)
+        asked = lax.rem(j // bit, 2)
+        found = found + bit * (mine + asked - 2 * mine * asked)
+        bit *= 2
+    return found
 
 
 def sweep_kernel(
@@ -248,19 +260,17 @@
         return parts[b].astype(BF16)
 
     if energies <= 8:
-        spread = product_of(lax.rem(me + 1, energies))
-        for j in range(1, energies + 1):
-            other = lax.rem(me + j, energies)
+        order = [partner(me, jnp.int32(j), energies) for j in range(energies - 1, 0, -1)]
+        spread = product_of(order[0])
+        for at, other in enumerate(order):
             current = spread
-            if j < energies:
-                spread = product_of(lax.rem(me + j + 1, energies))
-                sent[other] = pick(other, current)
-                exchange_one(other).start()
-            else:
-                held[REACH + me] = pick(me, current)
+            spread = product_of(order[at + 1] if at + 1 < len(order) else me)
+            sent[other] = pick(other, current)
+            exchange_one(other).start()
+        held[REACH + me] = pick(me, spread)
     else:
         def serve(j, carry):
-            other = lax.rem(me + j, energies)
+            other = partner(me, energies - j, energies)
             sent[other] = pick(other, product_of(other))
             exchange_one(other).start()
             return carry
@@ -269,7 +279,7 @@
         held[REACH + me] = pick(me, product_of(me))
 
     def await_one(j, carry):
-        other = lax.rem(me + j, energies)
+        other = partner(me, energies - j, energies)
         arrived(other, recv_one, held, REACH + other).wait_recv()
         return carry
 
@@ -283,14 +293,14 @@
     totals[...] = total.astype(BF16)
 
     def send_back(j, carry):
-        exchange_two(lax.rem(me + j, energies)).start()
+        exchange_two(partner(me, energies - j, energies)).start()
         return carry
 
     lax.fori_loop(1, energies, send_back, 0)
     gathered[me] = totals[me]
 
     def await_two(j, carry):
-        other = lax.rem(me + j, energies)
+        other = partner(me, energies - j, energies)
         arrived(other, recv_two, gathered, other).wait_recv()
         return carry
 
@@ -302,7 +312,7 @@
             ].astype(F32)
 
     def settle(j, carry):
-        other = lax.rem(me + j, energies)
+        other = partner(me, energies - j, energies)
         exchange_one(other).wait_send()
         exchange_two(other).wait_send()
         return carry

time: 25.3 us -> 24.4 us (0.964)
  Pallas kernels: 23.7 us -> 22.7 us
    pallas_call x1, Pallas kernels: 23.7 us -> 22.7 us  [on_device(): pl.pallas_call(functools.partial(sweep_kernel, energies, sections), out_s...]
where the time goes in v4:
time: 24.4 us; the launch traced here: 24.2 us
  Pallas kernels  22.7 us (93%)
  local copies, waits for them, and re-layouts  1.47 us (6%)
    pallas_call x1, Pallas kernels, on_device(): pl.pallas_call(functools.partial(sweep_kernel, energies, sections), out_s...  22.7 us
    unnamed x1, local copies, waits for them, and re-layouts  1.47 us

profile of v4, /device:TPU:0, one launch (start us, length us, event | category | flops | bytes accessed | tf_op | source)
XLA Modules:
  0.0 24.2 jit_solution(5785520084493326452)
XLA Ops:
  0.0 22.7 %shard_map.73 = f32[2,64,128]{2,1,0:T(8,128)} custom-call(bf16[2,384,384]{2,1,0:T(8,128)(2,1)} %bitcast.6, bf16[384,128]{1,0:T(8,128)(2,1)} %bitcast.8, bf16[384,128]{1,0:T(8,128)(2,1)} %bitcast.9, s32[64,128]{1,0:T(8,128)} %bitcast.10, s32[64,128]{1,0:T(8,128)} %bitcast.11, s32[8]{0:T(128)} %shift_ref.1, f32[8,8192]{1,0:T(8,128)} %coup_hbm.1), custom_call_target="tpu_custom_call" | custom-call | tf_op jit(solution)/shard_map/pallas_call | solution.py:349
  22.7 1.5 %copy.10 = f32[2,1,8192]{2,1,0:T(1,128)} copy(f32[2,1,8192]{2,1,0:T(1,128)} %bitcast.7) | data formatting | bytes 131072

commit v5 on v4

--- a/solution.py
+++ b/solution.py
@@ -87,10 +87,21 @@
             device_id={"section": to}, device_id_type=MESH,
         )
 
-    fwd_first = passed(fsrc_hbm, y_in, fwd_send, fwd_recv, after)
-    fwd = passed(y, y_in, fwd_send, fwd_recv, after)
-    bwd_first = passed(bsrc_hbm, w_end, end_send, end_recv, before)
-    bwd = passed(w_t, w_in, bwd_send, bwd_recv, before)
+    cuts = ((0, DEEP), (DEEP, orb))
+    fwd_first, fwd, bwd_first, bwd = [], [], [], []
+    for n, (low, high) in enumerate(cuts):
+        span = pl.ds(low, high - low)
+        fwd_first.append(
+            passed(fsrc_hbm.at[span], y_in.at[span], fwd_send.at[n], fwd_recv.at[n], after)
+        )
+        fwd.append(passed(y.at[span], y_in.at[span], fwd_send.at[n], fwd_recv.at[n], after))
+        bwd_first.append(
+            passed(bsrc_hbm.at[span], w_end.at[span], end_send.at[n], end_recv.at[n], before)
+        )
+        bwd.append(
+            passed(w_t.at[:, span], w_in.at[:, span], bwd_send.at[n], bwd_recv.at[n], before)
+        )
+
     base = s * orb
 
     def choose(b, carry):
@@ -105,11 +116,13 @@
 
     @pl.when(s == 0)
     def _():
-        fwd_first.start()
+        for piece in fwd_first:
+            piece.start()
 
     @pl.when(s == sections - 1)
     def _():
-        bwd_first.start()
+        for piece in bwd_first:
+            piece.start()
 
     for at in (0, 1, 2):
         loads[at].wait()
@@ -134,39 +147,63 @@
     def turn(t, carry):
         @pl.when(s == t)
         def _():
-            fwd.wait_recv()
-            current = y_in[...]
-            first = jnp.dot(prop[0], current, preferred_element_type=F32)
-            second = jnp.dot(prop[1], current, preferred_element_type=F32)
-            lane = lax.broadcasted_iota(jnp.int32, second.shape, 1)
-            crossed = pltpu.roll(second, half, 1)
-            crossed = jnp.where(lane < half, -crossed, crossed)
-            y[...] = (first + crossed + fsrc[...].astype(F32)).astype(BF16)
-
-            @pl.when(s < sections - 1)
-            def _():
-                fwd.start()
+            sums = [None, None]
+            for n, (low, high) in enumerate(cuts):
+                fwd[n].wait_recv()
+                current = y_in[low:high]
+                if n == 0:
+                    sums = [
+                        jnp.dot(prop[c, :, low:high], current, preferred_element_type=F32)
+                        for c in range(2)
+                    ]
+            lane = lax.broadcasted_iota(jnp.int32, (orb, cols), 1)
+            for n, (top, end) in enumerate(cuts):
+                first, second = [
+                    sums[c][top:end] + jnp.dot(
+                        prop[c, top:end, low:high], current, preferred_element_type=F32
+                    )
+                    for c in range(2)
+                ]
+                crossed = pltpu.roll(second, half, 1)
+                crossed = jnp.where(lane[top:end] < half, -crossed, crossed)
+                y[top:end] = (first + crossed + fsrc[top:end].astype(F32)).astype(BF16)
+
+                @pl.when(s < sections - 1)
+                def _(n=n):
+                    fwd[n].start()
 
         @pl.when(s == sections - 1 - t)
         def _():
-            @pl.when(t == 1)
-            def _():
-                bwd_first.wait_recv()
-                w_in[...] = w_end[...].astype(F32).T.astype(BF16)
-
-            @pl.when(t > 1)
-            def _():
-                bwd.wait_recv()
-
-            current = w_in[...]
-            first = jnp.dot(current, prop[0], preferred_element_type=F32)
-            second = jnp.dot(current, prop[1], preferred_element_type=F32)
-            crossed = jnp.concatenate([second[half:], -second[:half]], axis=0)
-            w_t[...] = (first + crossed + bsrc_t[...]).astype(BF16)
-
-            @pl.when(s > 0)
-            def _():
-                bwd.start()
+            sums = [None, None]
+            for n, (low, high) in enumerate(cuts):
+                @pl.when(t == 1)
+                def _(n=n, low=low, high=high):
+                    bwd_first[n].wait_recv()
+                    w_in[:, low:high] = w_end[low:high].astype(F32).T.astype(BF16)
+
+                @pl.when(t > 1)
+                def _(n=n):
+                    bwd[n].wait_recv()
+
+                current = w_in[:, low:high]
+                if n == 0:
+                    sums = [
+                        jnp.dot(current, prop[c, low:high, :], preferred_element_type=F32)
+                        for c in range(2)
+                    ]
+            for n, (top, end) in enumerate(cuts):
+                first, second = [
+                    sums[c][:, top:end] + jnp.dot(
+                        current, prop[c, low:high, top:end], preferred_element_type=F32
+                    )
+                    for c in range(2)
+                ]
+                crossed = jnp.concatenate([second[half:], -second[:half]], axis=0)
+                w_t[:, top:end] = (first + crossed + bsrc_t[:, top:end]).astype(BF16)
+
+                @pl.when(s > 0)
+                def _(n=n):
+                    bwd[n].start()
 
         @pl.when(t < sections - 1)
         def _():
@@ -321,15 +358,18 @@
 
     @pl.when(s < sections - 1)
     def _():
-        fwd.wait_send()
+        for piece in fwd:
+            piece.wait_send()
 
     @pl.when(s == sections - 1)
     def _():
-        bwd_first.wait_send()
+        for piece in bwd_first:
+            piece.wait_send()
 
     @pl.when((s > 0) & (s < sections - 1))
     def _():
-        bwd.wait_send()
+        for piece in bwd:
+            piece.wait_send()
 
 
 def on_device(
@@ -373,12 +413,12 @@
             pltpu.VMEM((energies, tall, LANES), BF16),
             pltpu.VMEM((energies, tall, LANES), BF16),
             pltpu.SemaphoreType.DMA((6,)),
-            pltpu.SemaphoreType.DMA,
-            pltpu.SemaphoreType.DMA,
-            pltpu.SemaphoreType.DMA,
-            pltpu.SemaphoreType.DMA,
-            pltpu.SemaphoreType.DMA,
-            pltpu.SemaphoreType.DMA,
+            pltpu.SemaphoreType.DMA((2,)),
+            pltpu.SemaphoreType.DMA((2,)),
+            pltpu.SemaphoreType.DMA((2,)),
+            pltpu.SemaphoreType.DMA((2,)),
+            pltpu.SemaphoreType.DMA((2,)),
+            pltpu.SemaphoreType.DMA((2,)),
             pltpu.SemaphoreType.DMA((energies,)),
             pltpu.SemaphoreType.DMA((energies,)),
             pltpu.SemaphoreType.DMA((energies,)),

time: 24.4 us -> 24.8 us (1.016)
  Pallas kernels: 22.7 us -> 23.1 us
    pallas_call x1, Pallas kernels: 22.7 us -> 23.1 us  [on_device(): pl.pallas_call(functools.partial(sweep_kernel, energies, sections), out_s...]
where the time goes in v5:
time: 24.8 us; the launch traced here: 24.6 us
  Pallas kernels  23.1 us (93%)
  local copies, waits for them, and re-layouts  1.47 us (6%)
    pallas_call x1, Pallas kernels, on_device(): pl.pallas_call(functools.partial(sweep_kernel, energies, sections), out_s...  23.1 us
    unnamed x1, local copies, waits for them, and re-layouts  1.47 us

profile of v5, /device:TPU:0, one launch (start us, length us, event | category | flops | bytes accessed | tf_op | source)
XLA Modules:
  0.0 24.6 jit_solution(6710935526549020131)
XLA Ops:
  0.0 23.1 %shard_map.73 = f32[2,64,128]{2,1,0:T(8,128)} custom-call(bf16[2,384,384]{2,1,0:T(8,128)(2,1)} %bitcast.6, bf16[384,128]{1,0:T(8,128)(2,1)} %bitcast.8, bf16[384,128]{1,0:T(8,128)(2,1)} %bitcast.9, s32[64,128]{1,0:T(8,128)} %bitcast.10, s32[64,128]{1,0:T(8,128)} %bitcast.11, s32[8]{0:T(128)} %shift_ref.1, f32[8,8192]{1,0:T(8,128)} %coup_hbm.1), custom_call_target="tpu_custom_call" | custom-call | tf_op jit(solution)/shard_map/pallas_call | solution.py:389
  23.1 1.5 %copy.10 = f32[2,1,8192]{2,1,0:T(1,128)} copy(f32[2,1,8192]{2,1,0:T(1,128)} %bitcast.7) | data formatting | bytes 131072
